TPU v7x, 32 devices: a whole 2x2x4 slice. The times are simulated.
32 devices in a mesh: runs: 2 (over y), tiles: 4 (over z), bands: 4 (over x, core).
Axes of the slice: x: 2, y: 2, z: 4, core: 2. Of those that a mesh axis runs over, the one named last changes fastest.
Arguments:
- spectra: float32 [48, 36, 128, 128], P('bands', None, ('runs', 'tiles')), parts along dimension 2, may hold values from 0.05 to 2
- sea_mask: int32 [128, 128], P('runs'), parts along dimension 0, may hold values from 0 to 1, as said below
- neighbors: int32 [4, 128, 128], P(None, ('runs', 'tiles')), parts along dimension 1, may hold values from 0 to 2304, as said below
- courant: float32 [128, 128], P(('runs', 'tiles')), parts along dimension 0, may hold values from 0.2 to 0.7
- turning: float32 [128, 128], P(('runs', 'tiles')), parts along dimension 0, may hold values from -0.3 to 0.3
- wind_speed: float32 [128, 128], P(('runs', 'tiles')), parts along dimension 0, may hold values from 0.2 to 1
- wind_dir: float32 [128, 128], P(('runs', 'tiles')), parts along dimension 0, may hold values from -3.140625 to 3.140625
Outputs:
- new_spectra: float32 [48, 36, 128, 128], P('bands', None, ('runs', 'tiles')), parts along dimension 2
There are 2 independent parts, one for each index of `runs`. A program takes and returns all parts, laid end to end along the dimension named above; each array names one. Nothing has to cross between parts.
Inputs may be any that keep to these rules, and one draw needn't show every extreme that they name: `sea_mask`: exactly 32 tiles hold one or more sea points, among them the first and the last tile of every block of 16 tiles; every point of the other tiles is land. neighbors[k, t, p] names the west (k = 0), east (1), south (2) and north (3) neighbour of point p of tile t as (tile - first tile of t's block of 16 tiles + 1) * 128 + point, where west and east lie in tile t, south in tile t - 1 and north in tile t + 1; (18) * 128 means no neighbour.
All inputs are finite; a program needn't handle non-finite values.
Results may differ from a plain program's by a relative error of at most 0.0003.
Values sent between devices are 32-bit elements; how exact they have to be, the bound alone decides.
A program may use at most 64 MiB of HBM per device.

v0:
```python
import math

import jax
import jax.numpy as jnp
from jax import lax
from jax.sharding import PartitionSpec as P


def extended_2(block, sides, width):
    for axis, dim in sides:
        count = lax.axis_size(axis)
        forward = [(i, i + 1) for i in range(count - 1)]
        backward = [(target, source) for source, target in forward]
        low = lax.ppermute(
            lax.slice_in_dim(block, block.shape[dim] - width, None, axis=dim), axis, forward
        )
        high = lax.ppermute(lax.slice_in_dim(block, 0, width, axis=dim), axis, backward)
        block = jnp.concatenate([low, block, high], axis=dim)
    return block


def directions_table(dir_count):
    angles = 2.0 * math.pi * (jnp.arange(dir_count).astype(jnp.float32) + 0.5) / dir_count
    return (jnp.cos(angles), jnp.sin(angles))


def select_points(extended, link_rows, offset, tiles_here, points):
    source_tiles = extended[:, :, offset : offset + tiles_here]
    tile_base = ((jnp.arange(tiles_here) + offset) * points)[:, None, None]
    point_ids = jnp.arange(points)[None, :, None]
    selector = (link_rows[:, None, :] - tile_base == point_ids).astype(jnp.float32)
    return jnp.einsum("bdtq,tqp->bdtp", source_tiles, selector, precision=lax.Precision.HIGHEST)


def propagate(
    spectrum, extended, link_table, sea_float, courant, turning, speed_ratio, cosines, sine_table
):
    band_width, dir_count, tiles_here, points = spectrum.shape
    west_side = select_points(extended, link_table[0], 1, tiles_here, points)
    east_side = select_points(extended, link_table[1], 1, tiles_here, points)
    south_side = select_points(extended, link_table[2], 0, tiles_here, points)
    north_side = select_points(extended, link_table[3], 2, tiles_here, points)
    group_speed = speed_ratio[:, None, None, None] * courant[None, None]
    along_x = group_speed * cosines[None, :, None, None]
    along_y = group_speed * sine_table[None, :, None, None]
    advected = (
        spectrum
        - jnp.maximum(along_x, 0.0) * (spectrum - west_side)
        - jnp.maximum(-along_x, 0.0) * (spectrum - east_side)
        - jnp.maximum(along_y, 0.0) * (spectrum - south_side)
        - jnp.maximum(-along_y, 0.0) * (spectrum - north_side)
    )
    advected = advected * sea_float[None, None]
    turn_rate = (0.5 + 0.5 * speed_ratio)[:, None, None, None] * turning[None, None]
    lower_dir = jnp.roll(advected, 1, axis=1)
    upper_dir = jnp.roll(advected, -1, axis=1)
    return (
        advected
        - jnp.maximum(turn_rate, 0.0) * (advected - lower_dir)
        - jnp.maximum(-turn_rate, 0.0) * (advected - upper_dir)
    )


def source_terms(spectrum, widened, steepness, fraction, wind_east, wind_north):
    band_width, dir_count = (spectrum.shape[0], spectrum.shape[1])
    cosines, sine_table = directions_table(dir_count)
    facing = (
        wind_east[None, None] * cosines[None, :, None, None]
        + wind_north[None, None] * sine_table[None, :, None, None]
    )
    growth = 0.5 * fraction * jnp.maximum(facing, 0.0)
    damping = (0.2 + fraction) * (steepness / (steepness + 1.0))[None, None]
    higher = widened[4:]
    lower_band = widened[:band_width]
    first_up = jnp.roll(higher, -3, axis=1)
    first_down = jnp.roll(lower_band, 3, axis=1)
    second_up = jnp.roll(higher, 3, axis=1)
    second_down = jnp.roll(lower_band, -3, axis=1)
    quadruplet = spectrum * spectrum * (
        first_up + first_down + second_up + second_down
    ) - 2.0 * spectrum * (first_up * first_down + second_up * second_down)
    return spectrum * jnp.exp(growth - damping) + 0.05 * (1.0 + fraction) * quadruplet


def sources(spectrum, wind_east, wind_north):
    freq_count, dir_count = (spectrum.shape[0], spectrum.shape[1])
    fraction = (jnp.arange(freq_count).astype(jnp.float32) / (freq_count - 1))[:, None, None, None]
    steepness = jnp.sum((0.5 + fraction) * spectrum, axis=(0, 1)) / (freq_count * dir_count)
    widened = jnp.pad(spectrum, ((2, 2), (0, 0), (0, 0), (0, 0)))
    return source_terms(spectrum, widened, steepness, fraction, wind_east, wind_north)


def band_step(spectrum, wind_pair):
    gathered = lax.all_to_all(spectrum, "bands", split_axis=2, concat_axis=0, tiled=True)
    wind_parts = lax.all_to_all(wind_pair, "bands", split_axis=2, concat_axis=0, tiled=True)
    updated = sources(gathered, wind_parts[0, 0], wind_parts[1, 0])
    return lax.all_to_all(updated, "bands", split_axis=0, concat_axis=2, tiled=True)


def per_device(spectra, sea_mask, neighbors, courant, turning, wind_speed, wind_dir):
    band_width, dir_count, tiles_here, points = spectra.shape
    tile_rank = lax.axis_index("tiles")
    band_rank = lax.axis_index("bands")
    first_tile = tile_rank * tiles_here
    sea_float = lax.dynamic_slice_in_dim(sea_mask, first_tile, tiles_here, 0).astype(jnp.float32)
    masked = spectra * sea_float[None, None]
    extended = extended_2(masked, (("tiles", 2),), 1)
    freq_index = band_rank * band_width + jnp.arange(band_width)
    speed_ratio = jnp.power(jnp.float32(1.1), -freq_index.astype(jnp.float32))
    cosines, sine_table = directions_table(dir_count)
    stepped = propagate(
        masked, extended, neighbors, sea_float, courant, turning, speed_ratio, cosines, sine_table
    )
    wind_pair = jnp.stack([wind_speed * jnp.cos(wind_dir), wind_speed * jnp.sin(wind_dir)])[:, None]
    result = band_step(stepped, wind_pair)
    return result


def solution(mesh):
    placed = (
        P("bands", None, ("runs", "tiles"), None),
        P("runs", None),
        P(None, ("runs", "tiles"), None),
        P(("runs", "tiles"), None),
        P(("runs", "tiles"), None),
        P(("runs", "tiles"), None),
        P(("runs", "tiles"), None),
    )
    return jax.shard_map(
        per_device,
        mesh=mesh,
        in_specs=placed,
        out_specs=P("bands", None, ("runs", "tiles"), None),
        check_vma=False,
    )
```

profile of v0, /device:TPU:0, one launch (start us, length us, event | category | flops | bytes accessed | tf_op | source)
XLA Modules:
  0.0 148.1 jit_solution(18122038529142569099)
XLA Ops:
  0.0 0.8 cosine_multiply_fusion
  0.8 0.6 maximum_bitcast_fusion
  1.4 4.2 %all-to-all-start.1 = ((f32[2,1,16,128]{3,0,1,2:T(2,128)}), f32[2,1,16,128]{3,0,1,2:T(2,128)}, u32[]{:S(2)}, u32[]{:S(2)}) async-start(f32[2,1,16,128]{3,0,1,2:T(2,128)} %maximum_bitcast_fusion), calls=%async_computation.1 | async-start | bytes 32768 | tf_op jit(solution)/shard_map/all_to_all | solution.py:95
  5.6 0.7 dynamic-slice_convert_fusion
  6.3 3.3 %copy_multiply_fusion = f32[12,36,16,128]{3,1,0,2:T(8,128)S(1)} fusion(f32[12,36,16,128]{3,2,1,0:T(8,128)} %param.7, f32[16,128]{1,0:T(8,128)S(1)} %dynamic-slice_convert_fusion), kind=kLoop, calls=%fused_computation.31 | loop fusion | flops 884736 | bytes 7086080 | tf_op jit(solution)/shard_map/mul | solution.py:106
  9.6 1.8 %copy-done = f32[12,36,16,128]{3,1,0,2:T(8,128)} copy-done((f32[12,36,16,128]{3,1,0,2:T(8,128)}, f32[12,36,16,128]{3,1,0,2:T(8,128)S(1)}, u32[]{:S(2)}) %copy-start) | copy-done | bytes 3538968
  11.5 0.8 fusion.42
  12.3 1.3 collective-permute-start.1
  13.6 5.9 %collective-permute-start = (f32[12,36,1,128]{3,1,0,2:T(8,128)}, f32[12,36,1,128]{3,1,0,2:T(8,128)}, u32[]{:S(2)}, u32[]{:S(2)}) collective-permute-start(f32[12,36,1,128]{3,1,0,2:T(8,128)} %get-tuple-element.12), channel_id=1, source_target_pairs={{0,4},{4,8},{8,12},{1,5},{5,9},{9,13},{2,6},{6,10},{10,14},{3,7},{... | collective-permute-start | bytes 663560 | tf_op jit(solution)/shard_map/ppermute | solution.py:14
  19.6 0.8 bitcast_subtract_fusion.7
  20.4 2.8 %fusion.21 = f32[16,128,12,36]{1,3,2,0:T(8,128)S(1)} fusion(s32[16,128]{1,0:T(8,128)S(1)} %get-tuple-element.21, f32[12,36,16,128]{3,2,1,0:T(8,128)S(1)} %copy-done.2, f32[16,128]{1,0:T(8,128)S(1)} %dynamic-slice_convert_fusion), kind=kOutput, calls=%fused_computation.52 | convolution fusion | flops 1360101376 | bytes 7094272 | tf_op jit(solution)/shard_map/bdtq,tqp->bdtp/dot_general | solution.py:32
  23.2 0.0 copy-start.3
  23.2 0.0 copy-start.4
  23.3 2.8 %fusion.24 = f32[16,128,12,36]{1,3,2,0:T(8,128)S(1)} fusion(s32[16,128]{1,0:T(8,128)S(1)} %get-tuple-element.22, f32[12,36,16,128]{3,2,1,0:T(8,128)S(1)} %copy-done.2, f32[16,128]{1,0:T(8,128)S(1)} %dynamic-slice_convert_fusion), kind=kOutput, calls=%fused_computation.54 | convolution fusion | flops 1360101376 | bytes 7094272 | tf_op jit(solution)/shard_map/bdtq,tqp->bdtp/dot_general | solution.py:32
  26.1 0.1 multiply_maximum_fusion.2
  26.2 0.1 broadcast_multiply_fusion
  26.3 3.0 %fusion.13 = f32[16,128,12,36]{1,3,2,0:T(8,128)S(1)} fusion(f32[12,36,16,128]{3,1,0,2:T(8,128)S(1)} %copy-done.1, f32[12,36,1,128]{3,1,0,2:T(8,128)} %collective-permute-done, s32[16,128]{1,0:T(8,128)S(1)} %get-tuple-element.24), kind=kOutput, calls=%fused_computation.19 | convolution fusion | flops 1360101376 | bytes 7307264 | tf_op jit(solution)/shard_map/bdtq,tqp->bdtp/dot_general | solution.py:32
  29.3 5.8 %fusion.5 = f32[12,36,16,128]{3,1,0,2:T(8,128)S(1)} fusion(f32[12,36,16,128]{3,1,0,2:T(8,128)S(1)} %copy-done.1, f32[16,128,12,36]{1,3,2,0:T(8,128)S(1)} %fusion.13, f32[16,128,12,36]{1,3,2,0:T(8,128)S(1)} %fusion.24, f32[16,128,12,36]{1,3,2,0:T(8,128)S(1)} %fusion.21, f32[12,36,1,128]{3,1,0,2:T(8,128)} %collective-permute-done.1, ...), kind=kOutput, calls=%fused_computation.9 | convolution fusion | flops 1378680832 | bytes 18030880 | tf_op jit(solution)/shard_map/bdtq,tqp->bdtp/dot_general | solution.py:32
  35.1 0.1 fusion.41
  35.3 0.8 fusion.40
  36.1 3.2 %fusion.17 = f32[12,36,16,128]{3,1,0,2:T(8,128)} fusion(f32[12,36,16,128]{3,1,0,2:T(8,128)S(1)} %fusion.5, f32[12,35,16,128]{3,1,0,2:T(8,128)S(1)} %get-tuple-element.8, f32[12,1,16,128]{3,1,0,2:T(1,128)S(1)} %get-tuple-element.10, f32[12,1,16,128]{3,1,0,2:T(1,128)S(1)} %get-tuple-element.9, f32[12,35,16,128]{3,1,0,2:T(8,128)S(1)} %get-tuple-element.7, ...), kind=kLoop, calls=%fused_computation.24 | loop fusion | flops 7077888 | bytes 14352384 | tf_op jit(solution)/shard_map/sub | solution.py:58
  39.3 4.8 %all-to-all-start = ((f32[12,36,16,128]{3,1,0,2:T(8,128)}), f32[12,36,16,128]{3,1,0,2:T(8,128)}, u32[]{:S(2)}, u32[]{:S(2)}) async-start(f32[12,36,16,128]{3,1,0,2:T(8,128)} %fusion.17), calls=%async_computation | async-start | bytes 7864320 | tf_op jit(solution)/shard_map/all_to_all | solution.py:94
  44.1 0.7 copy.18
  44.9 0.1 add_maximum_fusion
  45.0 44.5 %all-to-all-done = f32[12,36,16,128]{3,1,0,2:T(8,128)} async-done(((f32[12,36,16,128]{3,1,0,2:T(8,128)}), f32[12,36,16,128]{3,1,0,2:T(8,128)}, u32[]{:S(2)}, u32[]{:S(2)}) %all-to-all-start) | async-done | bytes 3538976 | tf_op jit(solution)/shard_map/all_to_all | solution.py:94
  89.5 5.1 %fusion.19 = (f32[4,128]{1,0:T(4,128)S(1)}, f32[12,36,4,4,128]{4,3,1,0,2:T(4,128)S(1)}) fusion(f32[4,12]{1,0:T(4,128)S(1)} %multiply_add_fusion.1, f32[12,36,4,4,128]{4,1,0,3,2:T(8,128)} %bitcast.16), kind=kLoop, calls=%fused_computation.37 | loop fusion | flops 1768960 | bytes 7080128 | tf_op jit(solution)/shard_map/reduce_sum | solution.py:88
  94.6 0.2 pad_slice_fusion.6
  94.8 1.5 %pad_slice_fusion.7 = (f32[48,33,4,128]{3,2,1,0:T(4,128)S(1)}, f32[48,33,4,128]{3,2,1,0:T(4,128)S(1)}, f32[48,33,4,128]{3,2,1,0:T(4,128)S(1)}, f32[48,33,4,128]{3,2,1,0:T(4,128)S(1)}) fusion(f32[48,36,4,128]{3,2,1,0:T(4,128)S(1)} %bitcast.67), kind=kLoop, calls=%fused_computation.46 | loop fusion | bytes 16515072 | tf_op jit(solution)/shard_map/jit(_roll_static)/slice | solution.py:75
  96.3 0.1 broadcast_multiply_fusion.1
  96.4 5.4 %multiply_add_fusion = f32[48,36,4,128]{3,2,1,0:T(4,128)S(1)} fusion(f32[48,3,4,128]{3,2,1,0:T(4,128)S(1)} %get-tuple-element.20, f32[48,33,4,128]{3,2,1,0:T(4,128)S(1)} %get-tuple-element.16, f32[48,33,4,128]{3,2,1,0:T(4,128)S(1)} %get-tuple-element.15, f32[48,3,4,128]{3,2,1,0:T(4,128)S(1)} %get-tuple-element.19, ...), kind=kLoop, calls=%fused_computation.38 | loop fusion | flops 17694720 | bytes 21406080 | tf_op jit(solution)/shard_map/add | solution.py:82
  101.8 43.7 %all_to_all.54 = f32[48,36,4,128]{3,2,1,0:T(4,128)S(1)} all-to-all(f32[48,36,4,128]{3,2,1,0:T(4,128)S(1)} %multiply_add_fusion), channel_id=1, replica_groups=mesh['runs'=2,'tiles'=4,'bands'=4] {'bands'}, dimensions={0} | all-to-all | bytes 7077888 | tf_op jit(solution)/shard_map/all_to_all | solution.py:97
  145.5 2.6 %copy.19 = f32[12,36,4,4,128]{4,3,2,1,0:T(4,128)} copy(f32[12,36,4,4,128]{4,3,1,0,2:T(4,128)S(1)} %bitcast.68) | data formatting | bytes 7077888 | tf_op jit(solution)/shard_map/all_to_all | solution.py:97
  (20 shorter events, 0.1 us)
Async XLA Ops:
  1.4 37.9 %all-to-all-start.1 = ((f32[2,1,16,128]{3,0,1,2:T(2,128)}), f32[2,1,16,128]{3,0,1,2:T(2,128)}, u32[]{:S(2)}, u32[]{:S(2)}) async-start(f32[2,1,16,128]{3,0,1,2:T(2,128)} %maximum_bitcast_fusion), calls=%async_computation.1 | async-start | bytes 32768 | tf_op jit(solution)/shard_map/all_to_all | solution.py:95
  6.3 14.1 %copy-start.2 = (f32[12,36,16,128]{3,2,1,0:T(8,128)S(1)}, f32[12,36,16,128]{3,2,1,0:T(8,128)}, u32[]{:S(2)}) copy-start(f32[12,36,16,128]{3,2,1,0:T(8,128)} %param.7) | copy-start | bytes 10616836
  9.6 1.9 %copy-start = (f32[12,36,16,128]{3,1,0,2:T(8,128)}, f32[12,36,16,128]{3,1,0,2:T(8,128)S(1)}, u32[]{:S(2)}) copy-start(f32[12,36,16,128]{3,1,0,2:T(8,128)S(1)} %copy_multiply_fusion) | copy-start | bytes 10616836
  12.3 17.0 %collective-permute-start.1 = (f32[12,36,1,128]{3,1,0,2:T(8,128)}, f32[12,36,1,128]{3,1,0,2:T(8,128)}, u32[]{:S(2)}, u32[]{:S(2)}) collective-permute-start(f32[12,36,1,128]{3,1,0,2:T(8,128)} %get-tuple-element.11), channel_id=1, source_target_pairs={{4,0},{8,4},{12,8},{5,1},{9,5},{13,9},{6,2},{10,6},{14,10},{7,3},{... | collective-permute-start | bytes 663560 | tf_op jit(solution)/shard_map/ppermute | solution.py:17
  13.6 12.7 %collective-permute-start = (f32[12,36,1,128]{3,1,0,2:T(8,128)}, f32[12,36,1,128]{3,1,0,2:T(8,128)}, u32[]{:S(2)}, u32[]{:S(2)}) collective-permute-start(f32[12,36,1,128]{3,1,0,2:T(8,128)} %get-tuple-element.12), channel_id=1, source_target_pairs={{0,4},{4,8},{8,12},{1,5},{5,9},{9,13},{2,6},{6,10},{10,14},{3,7},{... | collective-permute-start | bytes 663560 | tf_op jit(solution)/shard_map/ppermute | solution.py:14
  23.2 2.9 %copy-start.3 = (f32[16,128]{1,0:T(8,128)S(1)}, f32[16,128]{1,0:T(8,128)}, u32[]{:S(2)}) copy-start(f32[16,128]{1,0:T(8,128)} %param.11) | copy-start | bytes 24580
  23.2 3.0 %copy-start.4 = (f32[16,128]{1,0:T(8,128)S(1)}, f32[16,128]{1,0:T(8,128)}, u32[]{:S(2)}) copy-start(f32[16,128]{1,0:T(8,128)} %param.10) | copy-start | bytes 24580
  23.2 3.0 %copy-start.1 = (f32[12,36,16,128]{3,1,0,2:T(8,128)S(1)}, f32[12,36,16,128]{3,1,0,2:T(8,128)}, u32[]{:S(2)}) copy-start(f32[12,36,16,128]{3,1,0,2:T(8,128)} %copy-done) | copy-start | bytes 10616836
  39.3 50.2 %all-to-all-start = ((f32[12,36,16,128]{3,1,0,2:T(8,128)}), f32[12,36,16,128]{3,1,0,2:T(8,128)}, u32[]{:S(2)}, u32[]{:S(2)}) async-start(f32[12,36,16,128]{3,1,0,2:T(8,128)} %fusion.17), calls=%async_computation | async-start | bytes 7864320 | tf_op jit(solution)/shard_map/all_to_all | solution.py:94
where the time goes:
time: 149 us; the launch traced here: 148 us
  waiting for transfers between devices  44.5 us (30%)
  blocking collectives  43.7 us (29%)
  other arithmetic  20.4 us (14%)
  starting transfers between devices  16.2 us (11%)
  matrix products  14.4 us (10%)
  local copies, waits for them, and re-layouts  8.67 us (6%)
    all_to_all x1, waiting for transfers between devices, band_step(): lax.all_to_all(spectrum, 'bands', split_axis=2, concat_axis=0, tiled=True)  44.5 us
    all_to_all x1, blocking collectives, band_step(): lax.all_to_all(updated, 'bands', split_axis=0, concat_axis=2, tiled=True)  43.7 us
    dot_general x4, matrix products, select_points(): jnp.einsum('bdtq,tqp->bdtp', source_tiles, selector, precision=lax.Precis...  14.4 us
    ppermute x1, starting transfers between devices, extended_2(): lax.ppermute(lax.slice_in_dim(block, block.shape[dim] - width, None, axis...  5.91 us
    add x1, other arithmetic, source_terms(): spectrum * jnp.exp(growth - damping) + 0.05 * (1.0 + fraction) * quadruplet  5.38 us
    reduce_sum x1, other arithmetic, sources(): jnp.sum((0.5 + fraction) * spectrum, axis=(0, 1)) / (freq_count * dir_count)  5.09 us
    all_to_all x1, starting transfers between devices, band_step(): lax.all_to_all(spectrum, 'bands', split_axis=2, concat_axis=0, tiled=True)  4.79 us
    all_to_all x1, starting transfers between devices, band_step(): lax.all_to_all(wind_pair, 'bands', split_axis=2, concat_axis=0, tiled=True)  4.21 us
  transfers between devices with their start and end apart: 4, of which 1 were waited for; matrix products, arithmetic and copies ran while one was open for 17% of the time, Pallas kernels for 0%

commit v1 on v0

v1 whole, which is shorter than its diff:
```python
import functools
import math

import jax
import jax.numpy as jnp
from jax import lax
from jax.experimental import pallas as pl
from jax.experimental.pallas import tpu as pltpu
from jax.sharding import PartitionSpec as P

MESH = pl.DeviceIdType.MESH
F32 = jnp.float32
LOG2E = 1.0 / math.log(2.0)
GROUP = 2


def lane_gather(x, idx):
    return jnp.take_along_axis(x, idx, axis=1, mode="promise_in_bounds")


def sin_cos(angle):
    y = 0.5 * angle
    z = y * y
    s = 1.0
    for n in (12, 10, 8, 6, 4, 2):
        s = 1.0 - z * s * (1.0 / (n * (n + 1)))
    c = 1.0
    for n in (13, 11, 9, 7, 5, 3, 1):
        c = 1.0 - z * c * (1.0 / (n * (n + 1)))
    s = s * y
    return 2.0 * s * c, 1.0 - 2.0 * s * s


def kernel(
    n_bands, n_tiles, bw, nd, tp, width,
    spectra, mask, nbr, courant, turning, wspeed, wdir, out,
    ext, e1, e2, obuf, ftab, mext, weights, lanes, hsend, hrecv, macc, mrecv,
    load_sem, out_sem, band_send, band_recv, tile_send, tile_recv,
    diag_send, diag_recv, m_send, m_recv,
):
    band = lax.axis_index("bands")
    tile = lax.axis_index("tiles")
    groups = bw // GROUP
    grows = GROUP * nd
    rows = tp + 16
    nf = n_bands * bw
    flat = ext.reshape((bw + 4) * nd * rows, width)
    has_tile = (tile > 0, tile < n_tiles - 1)
    has_band = (band > 0, band < n_bands - 1)
    step = (-1, 1)

    def load(i):
        return pltpu.make_async_copy(
            spectra.at[i], ext.at[i + 2, :, 8 : 8 + tp, :], load_sem.at[i]
        )

    for i in range(bw):
        load(i).start()

    barrier = pltpu.get_barrier_semaphore()
    for k in range(1, n_bands):
        pl.semaphore_signal(
            barrier, inc=1, device_id={"bands": lax.rem(band + k, n_bands)}, device_id_type=MESH
        )
    for dt in (1, n_tiles - 1):
        for db in (0, 1, n_bands - 1):
            pl.semaphore_signal(
                barrier, inc=1,
                device_id={
                    "bands": lax.rem(band + db, n_bands), "tiles": lax.rem(tile + dt, n_tiles)
                },
                device_id_type=MESH,
            )
    pl.semaphore_wait(barrier, n_bands - 1 + 6)

    def band_copy(side):
        first, place = (bw - 2, 0) if side == 0 else (0, bw + 2)
        return pltpu.make_async_remote_copy(
            src_ref=spectra.at[first : first + 2],
            dst_ref=ext.at[place : place + 2, :, 8 : 8 + tp, :],
            send_sem=band_send.at[side], recv_sem=band_recv.at[side],
            device_id={"bands": band - step[side]}, device_id_type=MESH,
        )

    def tile_copy(side, g):
        first = pl.multiple_of(g * grows, 8)
        return pltpu.make_async_remote_copy(
            src_ref=hsend.at[side, pl.ds(first, grows), :],
            dst_ref=hrecv.at[side, pl.ds(first + 2 * nd, grows), :],
            send_sem=tile_send.at[side, g], recv_sem=tile_recv.at[side, g],
            device_id={"tiles": tile - step[side]}, device_id_type=MESH,
        )

    def diag_copy(bside, side):
        first, place = ((bw - 2) * nd, 0) if bside == 0 else (0, (bw + 2) * nd)
        return pltpu.make_async_remote_copy(
            src_ref=hsend.at[side, pl.ds(first, 2 * nd), :],
            dst_ref=hrecv.at[side, pl.ds(place, 2 * nd), :],
            send_sem=diag_send.at[bside, side], recv_sem=diag_recv.at[bside, side],
            device_id={"bands": band - step[bside], "tiles": tile - step[side]},
            device_id_type=MESH,
        )

    def m_copy(k):
        return pltpu.make_async_remote_copy(
            src_ref=macc, dst_ref=mrecv.at[k],
            send_sem=m_send.at[k], recv_sem=m_recv.at[k],
            device_id={"bands": lax.rem(band + k, n_bands)}, device_id_type=MESH,
        )

    for side in (0, 1):
        @pl.when(has_band[1 - side])
        def _(side=side):
            band_copy(side).start()

    for g in range(groups):
        for i in range(g * GROUP, (g + 1) * GROUP):
            load(i).wait()
        base = (g * GROUP + 2) * nd * rows
        for side, row in ((0, 8 + tp - 1), (1, 8)):
            hsend[side, pl.ds(g * grows, grows), :] = flat[pl.ds(base + row, grows, stride=rows), :]
            @pl.when(has_tile[1 - side])
            def _(side=side, g=g):
                tile_copy(side, g).start()
    for side in (0, 1):
        for bside in (0, 1):
            @pl.when(has_tile[1 - side] & has_band[1 - bside])
            def _(side=side, bside=bside):
                diag_copy(bside, side).start()

    first_tile = tile * tp
    below = pl.multiple_of(jnp.maximum(first_tile - 8, 0), 8)
    above = pl.multiple_of(jnp.minimum(first_tile + tp, n_tiles * tp - 8), 8)
    mext[0:8, :] = mask[pl.ds(below, 8), :].astype(F32) * jnp.where(tile > 0, 1.0, 0.0)
    mext[8 : 8 + tp, :] = mask[pl.ds(pl.multiple_of(first_tile, 8), tp), :].astype(F32)
    mext[8 + tp :, :] = mask[pl.ds(above, 8), :].astype(F32) * jnp.where(
        tile < n_tiles - 1, 1.0, 0.0
    )
    for side in (0, 1):
        @pl.when(jnp.logical_not(has_tile[side]))
        def _(side=side):
            hrecv[side] = jnp.zeros(hrecv.shape[1:], F32)
    shifts = (0, 0, -1, 1)
    for h in range(0, tp, 8):
        here = pl.ds(h, 8)
        own = mext[8 + h : 16 + h, :]
        cm = courant[here, :] * own
        for d in range(4):
            link = nbr[d, here, :]
            lane = jnp.bitwise_and(link, width - 1)
            there = lane_gather(mext[8 + h + shifts[d] : 16 + h + shifts[d], :], lane)
            lanes[d, here, :] = lane
            weights[d, here, :] = cm * jnp.where(link < (tp + 2) * width, there, 0.0)
        weights[4, here, :] = cm
        sw, cw = sin_cos(wdir[here, :])
        east, north = wspeed[here, :] * cw, wspeed[here, :] * sw
        for j in range(nd):
            angle = 2.0 * math.pi * (j + 0.5) / nd
            facing = east * math.cos(angle) + north * math.sin(angle)
            ftab[j, here, :] = (0.5 * LOG2E) * jnp.maximum(facing, 0.0)
    macc[...] = jnp.zeros(macc.shape, F32)

    quarter = nd // 4

    def advance(e, summed):
        index = (band * bw + e - 2).astype(F32)
        fraction = index * (1.0 / (nf - 1))
        ratio = jnp.exp(jnp.full((8, width), index, F32) * (-math.log(1.1)))
        for h in range(0, tp, 8):
            here = pl.ds(h, 8)
            own = mext[8 + h : 16 + h, :]
            lane = [lanes[d, here, :] for d in range(4)]
            weight = [weights[d, here, :] * ratio for d in range(4)]
            rcm = weights[4, here, :] * ratio
            total = None
            for k in range(quarter):
                angle = 2.0 * math.pi * (k + 0.5) / nd
                c, s = math.cos(angle), math.sin(angle)
                wx = (weight[0] * c, weight[1] * c)
                wy = (weight[2] * s, weight[3] * s)
                centre = own - rcm * (c + s)
                for j, x, y in (
                    (k, 0, 0), (nd // 2 - 1 - k, 1, 0), (nd // 2 + k, 1, 1), (nd - 1 - k, 0, 1)
                ):
                    mid = ext[e, j, 8 + h : 16 + h, :]
                    off = 8 + h + (1 if y else -1)
                    beside = ext[e, j, off : off + 8, :]
                    value = (
                        centre * mid
                        + wx[x] * lane_gather(mid, lane[x])
                        + wy[y] * lane_gather(beside, lane[2 + y])
                    )
                    e1[j, here, :] = value
                    total = value if total is None else total + value
            if summed:
                macc[here, :] += (0.5 + fraction) * total
            turn = turning[here, :]
            amount = jnp.abs(turn * (0.5 + 0.5 * ratio))
            lower = turn > 0.0
            prev, now = e1[nd - 1, here, :], e1[0, here, :]
            first = now
            for j in range(nd):
                after = e1[j + 1, here, :] if j < nd - 1 else first
                e2[e, j, here, :] = now + amount * (jnp.where(lower, prev, after) - now)
                prev, now = now, after

    def fill_edges(e, count):
        first = pl.multiple_of(e * nd, 4)
        for side, row in ((0, 7), (1, 8 + tp)):
            flat[pl.ds(e * nd * rows + row, count * nd, stride=rows), :] = hrecv[
                side, pl.ds(first, count * nd), :
            ]

    def own_group(g, carry):
        for side in (0, 1):
            @pl.when(has_tile[side])
            def _(side=side):
                tile_copy(side, g).wait_recv()
        fill_edges(2 + g * GROUP, GROUP)

        def one(u, c):
            advance(2 + g * GROUP + u, True)
            return c

        return lax.fori_loop(0, GROUP, one, carry)

    lax.fori_loop(0, groups, own_group, 0)

    for k in range(1, n_bands):
        m_copy(k).start()

    for bside, place in ((0, 0), (1, bw + 2)):
        @pl.when(has_band[bside])
        def _(bside=bside, place=place):
            band_copy(bside).wait_recv()
            for side in (0, 1):
                @pl.when(has_tile[side])
                def _(side=side):
                    diag_copy(bside, side).wait_recv()
            fill_edges(place, 2)

            def one(u, c):
                advance(place + u, False)
                return c

            lax.fori_loop(0, 2, one, 0)

        @pl.when(jnp.logical_not(has_band[bside]))
        def _(place=place):
            e2[place : place + 2] = jnp.zeros((2,) + e2.shape[1:], F32)

    m_sum = macc[...]
    for k in range(1, n_bands):
        m_copy(k).wait()
        m_sum = m_sum + mrecv[k]
    m_sum = m_sum * (1.0 / (nf * nd))
    mrecv[0] = LOG2E * (m_sum / (m_sum + 1.0))

    def store(i):
        return pltpu.make_async_copy(obuf.at[i], out.at[i], out_sem.at[i])

    def finish(i, carry):
        index = (band * bw + i).astype(F32)
        fraction = index * (1.0 / (nf - 1))
        k = 0.05 * (1.0 + fraction)
        for h in range(0, tp, 8):
            here = pl.ds(h, 8)
            damping = (0.2 + fraction) * mrecv[0, here, :]
            for j in range(nd):
                up, down = (j + 3) % nd, (j - 3) % nd
                a1, a2 = e2[i + 4, up, here, :], e2[i + 4, down, here, :]
                b1, b2 = e2[i, down, here, :], e2[i, up, here, :]
                mid = e2[i + 2, j, here, :]
                gain = jnp.exp2(fraction * ftab[j, here, :] - damping)
                inner = mid * ((a1 + b1) + (a2 + b2)) - 2.0 * (a1 * b1 + a2 * b2)
                obuf[i, j, here, :] = mid * (gain + k * inner)
        store(i).start()
        return carry

    lax.fori_loop(0, bw, finish, 0)

    for i in range(bw):
        store(i).wait()
    for side in (0, 1):
        @pl.when(has_band[1 - side])
        def _(side=side):
            band_copy(side).wait_send()

        @pl.when(has_tile[1 - side])
        def _(side=side):
            for g in range(groups):
                tile_copy(side, g).wait_send()

        for bside in (0, 1):
            @pl.when(has_tile[1 - side] & has_band[1 - bside])
            def _(side=side, bside=bside):
                diag_copy(bside, side).wait_send()


def solution(mesh):
    n_bands, n_tiles = mesh.shape["bands"], mesh.shape["tiles"]

    def per_device(spectra, sea_mask, neighbors, courant, turning, wind_speed, wind_dir):
        bw, nd, tp, width = spectra.shape
        vmem = pl.BlockSpec(memory_space=pltpu.VMEM)
        hbm = pl.BlockSpec(memory_space=pl.ANY)
        groups = bw // GROUP
        dma = pltpu.SemaphoreType.DMA
        return pl.pallas_call(
            functools.partial(kernel, n_bands, n_tiles, bw, nd, tp, width),
            out_shape=jax.ShapeDtypeStruct(spectra.shape, F32),
            in_specs=[hbm] + [vmem] * 6,
            out_specs=hbm,
            scratch_shapes=[
                pltpu.VMEM((bw + 4, nd, tp + 16, width), F32),
                pltpu.VMEM((nd, tp, width), F32),
                pltpu.VMEM((bw + 4, nd, tp, width), F32),
                pltpu.VMEM((bw, nd, tp, width), F32),
                pltpu.VMEM((nd, tp, width), F32),
                pltpu.VMEM((tp + 16, width), F32),
                pltpu.VMEM((5, tp, width), F32),
                pltpu.VMEM((4, tp, width), jnp.int32),
                pltpu.VMEM((2, bw * nd, width), F32),
                pltpu.VMEM((2, (bw + 4) * nd, width), F32),
                pltpu.VMEM((tp, width), F32),
                pltpu.VMEM((n_bands, tp, width), F32),
                dma((bw,)), dma((bw,)), dma((2,)), dma((2,)),
                dma((2, groups)), dma((2, groups)),
                dma((2, 2)), dma((2, 2)), dma((n_bands,)), dma((n_bands,)),
            ],
            compiler_params=pltpu.CompilerParams(
                collective_id=0, has_side_effects=True, vmem_limit_bytes=40 * 1024 * 1024
            ),
        )(spectra, sea_mask, neighbors, courant, turning, wind_speed, wind_dir)

    placed = (
        P("bands", None, ("runs", "tiles"), None),
        P("runs", None),
        P(None, ("runs", "tiles"), None),
        P(("runs", "tiles"), None),
        P(("runs", "tiles"), None),
        P(("runs", "tiles"), None),
        P(("runs", "tiles"), None),
    )
    return jax.shard_map(
        per_device,
        mesh=mesh,
        in_specs=placed,
        out_specs=P("bands", None, ("runs", "tiles"), None),
        check_vma=False,
    )
```

time: 149 us -> 27.8 us (0.19)
  waiting for transfers between devices: 44.5 us -> 0 us
  blocking collectives: 43.7 us -> 0 us
  other arithmetic: 20.4 us -> 0 us
  Pallas kernels: 0 us -> 19.3 us
  starting transfers between devices: 16.2 us -> 0 us
  matrix products: 14.4 us -> 0 us
    all_to_all x2 -> x0, waiting for transfers between devices: 44.5 us -> none  [the longest x1 44.5 us: band_step(): lax.all_to_all(spectrum, 'bands', split_axis=2, concat_axis=0, tiled=True)]
    all_to_all x1 -> x0, blocking collectives: 43.7 us -> none  [band_step(): lax.all_to_all(updated, 'bands', split_axis=0, concat_axis=2, tiled=True)]
    pallas_call x0 -> x1, Pallas kernels: none -> 19.3 us  [per_device(): pl.pallas_call(functools.partial(kernel, n_bands, n_tiles, bw, nd, tp, wi...]
    dot_general x4 -> x0, matrix products: 14.4 us -> none  [select_points(): jnp.einsum('bdtq,tqp->bdtp', source_tiles, selector, precision=lax.Precis...]
    all_to_all x2 -> x0, starting transfers between devices: 8.99 us -> none  [the longest x1 4.79 us: band_step(): lax.all_to_all(spectrum, 'bands', split_axis=2, concat_axis=0, tiled=True)]
    ppermute x2 -> x0, starting transfers between devices: 7.19 us -> none  [the longest x1 5.91 us: extended_2(): lax.ppermute(lax.slice_in_dim(block, block.shape[dim] - width, None, axis...]
    unnamed x10 -> x15, local copies, waits for them, and re-layouts: 1.87 us -> 8.1 us
    add x4 -> x0, other arithmetic: 5.41 us -> none  [the longest x1 5.38 us: source_terms(): spectrum * jnp.exp(growth - damping) + 0.05 * (1.0 + fraction) * quadruplet]
  transfers between devices with their start and end apart: 4 -> 0, of which waited for: 1 -> 0; matrix products, arithmetic and copies ran while one was open for 17% -> 0% of each run, Pallas kernels for 0% -> 0%
where the time goes in v1:
time: 27.8 us; the launch traced here: 27.4 us
  Pallas kernels  19.3 us (69%)
  local copies, waits for them, and re-layouts  8.1 us (29%)
    pallas_call x1, Pallas kernels, per_device(): pl.pallas_call(functools.partial(kernel, n_bands, n_tiles, bw, nd, tp, wi...  19.3 us
    unnamed x15, local copies, waits for them, and re-layouts  8.1 us

profile of v1, /device:TPU:0, one launch (start us, length us, event | category | flops | bytes accessed | tf_op | source)
XLA Modules:
  0.0 27.4 jit_solution(17321206278355344649)
XLA Ops:
  0.0 0.0 copy-start
  0.0 2.0 %copy-done = f32[12,36,16,128]{3,2,1,0:T(8,128)S(1)} copy-done((f32[12,36,16,128]{3,2,1,0:T(8,128)S(1)}, f32[12,36,16,128]{3,2,1,0:T(8,128)}, u32[]{:S(2)}) %copy-start) | copy-done | bytes 3538968
  2.0 0.0 copy-start.1
  2.0 0.8 %copy-done.1 = s32[64,128]{1,0:T(8,128)S(1)} copy-done((s32[64,128]{1,0:T(8,128)S(1)}, s32[64,128]{1,0:T(8,128)}, u32[]{:S(2)}) %copy-start.1) | copy-done | bytes 32792
  2.8 0.0 copy-start.2
  2.8 0.8 %copy-done.2 = s32[4,16,128]{2,1,0:T(8,128)S(1)} copy-done((s32[4,16,128]{2,1,0:T(8,128)S(1)}, s32[4,16,128]{2,1,0:T(8,128)}, u32[]{:S(2)}) %copy-start.2) | copy-done | bytes 32792
  3.5 0.0 copy-start.3
  3.5 0.7 %copy-done.3 = f32[16,128]{1,0:T(8,128)S(1)} copy-done((f32[16,128]{1,0:T(8,128)S(1)}, f32[16,128]{1,0:T(8,128)}, u32[]{:S(2)}) %copy-start.3) | copy-done | bytes 8216
  4.2 0.0 copy-start.4
  4.2 0.7 %copy-done.4 = f32[16,128]{1,0:T(8,128)S(1)} copy-done((f32[16,128]{1,0:T(8,128)S(1)}, f32[16,128]{1,0:T(8,128)}, u32[]{:S(2)}) %copy-start.4) | copy-done | bytes 8216
  4.9 0.0 copy-start.5
  4.9 0.7 %copy-done.5 = f32[16,128]{1,0:T(8,128)S(1)} copy-done((f32[16,128]{1,0:T(8,128)S(1)}, f32[16,128]{1,0:T(8,128)}, u32[]{:S(2)}) %copy-start.5) | copy-done | bytes 8216
  5.6 0.0 copy-start.6
  5.6 0.7 %copy-done.6 = f32[16,128]{1,0:T(8,128)S(1)} copy-done((f32[16,128]{1,0:T(8,128)S(1)}, f32[16,128]{1,0:T(8,128)}, u32[]{:S(2)}) %copy-start.6) | copy-done | bytes 8216
  6.3 19.3 %shard_map.73 = f32[12,36,16,128]{3,2,1,0:T(8,128)S(1)} custom-call(f32[12,36,16,128]{3,2,1,0:T(8,128)S(1)} %copy-done, s32[64,128]{1,0:T(8,128)S(1)} %copy-done.1, s32[4,16,128]{2,1,0:T(8,128)S(1)} %copy-done.2, f32[16,128]{1,0:T(8,128)S(1)} %copy-done.3, f32[16,128]{1,0:T(8,128)S(1)} %copy-done.4, f32[16,128]{1,0:T(8,128)S(1)} %copy-done.5, ...), custom_call_target="tpu_custom_call" | custom-call | tf_op jit(solution)/shard_map/pallas_call | solution.py:309
  25.6 1.8 %copy.9 = f32[12,36,16,128]{3,2,1,0:T(8,128)} copy(f32[12,36,16,128]{3,2,1,0:T(8,128)S(1)} %shard_map.73) | data formatting | bytes 7077888
Async XLA Ops:
  0.0 2.0 %copy-start = (f32[12,36,16,128]{3,2,1,0:T(8,128)S(1)}, f32[12,36,16,128]{3,2,1,0:T(8,128)}, u32[]{:S(2)}) copy-start(f32[12,36,16,128]{3,2,1,0:T(8,128)} %spectra.1) | copy-start | bytes 10616836
  2.0 0.8 %copy-start.1 = (s32[64,128]{1,0:T(8,128)S(1)}, s32[64,128]{1,0:T(8,128)}, u32[]{:S(2)}) copy-start(s32[64,128]{1,0:T(8,128)} %mask.1) | copy-start | bytes 98308
  2.8 0.8 %copy-start.2 = (s32[4,16,128]{2,1,0:T(8,128)S(1)}, s32[4,16,128]{2,1,0:T(8,128)}, u32[]{:S(2)}) copy-start(s32[4,16,128]{2,1,0:T(8,128)} %nbr.1) | copy-start | bytes 98308
  3.5 0.7 %copy-start.3 = (f32[16,128]{1,0:T(8,128)S(1)}, f32[16,128]{1,0:T(8,128)}, u32[]{:S(2)}) copy-start(f32[16,128]{1,0:T(8,128)} %courant.1) | copy-start | bytes 24580
  4.2 0.7 %copy-start.4 = (f32[16,128]{1,0:T(8,128)S(1)}, f32[16,128]{1,0:T(8,128)}, u32[]{:S(2)}) copy-start(f32[16,128]{1,0:T(8,128)} %turning.1) | copy-start | bytes 24580
  4.9 0.7 %copy-start.5 = (f32[16,128]{1,0:T(8,128)S(1)}, f32[16,128]{1,0:T(8,128)}, u32[]{:S(2)}) copy-start(f32[16,128]{1,0:T(8,128)} %wspeed.1) | copy-start | bytes 24580
  5.6 0.7 %copy-start.6 = (f32[16,128]{1,0:T(8,128)S(1)}, f32[16,128]{1,0:T(8,128)}, u32[]{:S(2)}) copy-start(f32[16,128]{1,0:T(8,128)} %wdir.1) | copy-start | bytes 24580

commit v2 on v1

--- a/solution.py
+++ b/solution.py
@@ -33,9 +33,9 @@
 
 def kernel(
     n_bands, n_tiles, bw, nd, tp, width,
-    spectra, mask, nbr, courant, turning, wspeed, wdir, out,
-    ext, e1, e2, obuf, ftab, mext, weights, lanes, hsend, hrecv, macc, mrecv,
-    load_sem, out_sem, band_send, band_recv, tile_send, tile_recv,
+    spectra, mask_in, nbr_in, courant_in, turning_in, wspeed_in, wdir_in, out,
+    mask, nbr, courant, turning, wspeed, wdir, ext, e1, e2, obuf, ftab, mext, weights, lanes, hsend, hrecv, macc, mrecv,
+    small_sem, load_sem, out_sem, band_send, band_recv, tile_send, tile_recv,
     diag_send, diag_recv, m_send, m_recv,
 ):
     band = lax.axis_index("bands")
@@ -54,8 +54,17 @@
             spectra.at[i], ext.at[i + 2, :, 8 : 8 + tp, :], load_sem.at[i]
         )
 
+    small = [
+        pltpu.make_async_copy(source, place, small_sem.at[n])
+        for n, (source, place) in enumerate((
+            (mask_in, mask), (nbr_in, nbr), (courant_in, courant),
+            (turning_in, turning), (wspeed_in, wspeed), (wdir_in, wdir),
+        ))
+    ]
     for i in range(bw):
         load(i).start()
+    for copy in small:
+        copy.start()
 
     barrier = pltpu.get_barrier_semaphore()
     for k in range(1, n_bands):
@@ -128,6 +137,8 @@
             def _(side=side, bside=bside):
                 diag_copy(bside, side).start()
 
+    for copy in small:
+        copy.wait()
     first_tile = tile * tp
     below = pl.multiple_of(jnp.maximum(first_tile - 8, 0), 8)
     above = pl.multiple_of(jnp.minimum(first_tile + tp, n_tiles * tp - 8), 8)
@@ -302,16 +313,21 @@
 
     def per_device(spectra, sea_mask, neighbors, courant, turning, wind_speed, wind_dir):
         bw, nd, tp, width = spectra.shape
-        vmem = pl.BlockSpec(memory_space=pltpu.VMEM)
-        hbm = pl.BlockSpec(memory_space=pl.ANY)
+        hbm = pl.BlockSpec(memory_space=pltpu.HBM)
         groups = bw // GROUP
         dma = pltpu.SemaphoreType.DMA
         return pl.pallas_call(
             functools.partial(kernel, n_bands, n_tiles, bw, nd, tp, width),
             out_shape=jax.ShapeDtypeStruct(spectra.shape, F32),
-            in_specs=[hbm] + [vmem] * 6,
+            in_specs=[hbm] * 7,
             out_specs=hbm,
             scratch_shapes=[
+                pltpu.VMEM(sea_mask.shape, jnp.int32),
+                pltpu.VMEM(neighbors.shape, jnp.int32),
+                pltpu.VMEM((tp, width), F32),
+                pltpu.VMEM((tp, width), F32),
+                pltpu.VMEM((tp, width), F32),
+                pltpu.VMEM((tp, width), F32),
                 pltpu.VMEM((bw + 4, nd, tp + 16, width), F32),
                 pltpu.VMEM((nd, tp, width), F32),
                 pltpu.VMEM((bw + 4, nd, tp, width), F32),
@@ -324,7 +340,7 @@
                 pltpu.VMEM((2, (bw + 4) * nd, width), F32),
                 pltpu.VMEM((tp, width), F32),
                 pltpu.VMEM((n_bands, tp, width), F32),
-                dma((bw,)), dma((bw,)), dma((2,)), dma((2,)),
+                dma((6,)), dma((bw,)), dma((bw,)), dma((2,)), dma((2,)),
                 dma((2, groups)), dma((2, groups)),
                 dma((2, 2)), dma((2, 2)), dma((n_bands,)), dma((n_bands,)),
             ],

time: 27.8 us -> 28 us (level)
  no operation moved by 1% of the time
where the time goes in v2:
time: 28 us; the launch traced here: 27.6 us
  Pallas kernels  19.4 us (69%)
  local copies, waits for them, and re-layouts  8.1 us (29%)
    pallas_call x1, Pallas kernels, per_device(): pl.pallas_call(functools.partial(kernel, n_bands, n_tiles, bw, nd, tp, wi...  19.4 us
    unnamed x15, local copies, waits for them, and re-layouts  8.1 us

profile of v2, /device:TPU:0, one launch (start us, length us, event | category | flops | bytes accessed | tf_op | source)
XLA Modules:
  0.0 27.6 jit_solution(10303926721143034477)
XLA Ops:
  0.0 0.0 copy-start
  0.0 2.0 %copy-done = f32[12,36,16,128]{3,2,1,0:T(8,128)S(1)} copy-done((f32[12,36,16,128]{3,2,1,0:T(8,128)S(1)}, f32[12,36,16,128]{3,2,1,0:T(8,128)}, u32[]{:S(2)}) %copy-start) | copy-done | bytes 3538968
  2.0 0.0 copy-start.1
  2.0 0.8 %copy-done.1 = s32[64,128]{1,0:T(8,128)S(1)} copy-done((s32[64,128]{1,0:T(8,128)S(1)}, s32[64,128]{1,0:T(8,128)}, u32[]{:S(2)}) %copy-start.1) | copy-done | bytes 32792
  2.8 0.0 copy-start.2
  2.8 0.8 %copy-done.2 = s32[4,16,128]{2,1,0:T(8,128)S(1)} copy-done((s32[4,16,128]{2,1,0:T(8,128)S(1)}, s32[4,16,128]{2,1,0:T(8,128)}, u32[]{:S(2)}) %copy-start.2) | copy-done | bytes 32792
  3.5 0.0 copy-start.3
  3.5 0.7 %copy-done.3 = f32[16,128]{1,0:T(8,128)S(1)} copy-done((f32[16,128]{1,0:T(8,128)S(1)}, f32[16,128]{1,0:T(8,128)}, u32[]{:S(2)}) %copy-start.3) | copy-done | bytes 8216
  4.2 0.0 copy-start.4
  4.2 0.7 %copy-done.4 = f32[16,128]{1,0:T(8,128)S(1)} copy-done((f32[16,128]{1,0:T(8,128)S(1)}, f32[16,128]{1,0:T(8,128)}, u32[]{:S(2)}) %copy-start.4) | copy-done | bytes 8216
  4.9 0.0 copy-start.5
  4.9 0.7 %copy-done.5 = f32[16,128]{1,0:T(8,128)S(1)} copy-done((f32[16,128]{1,0:T(8,128)S(1)}, f32[16,128]{1,0:T(8,128)}, u32[]{:S(2)}) %copy-start.5) | copy-done | bytes 8216
  5.6 0.0 copy-start.6
  5.6 0.7 %copy-done.6 = f32[16,128]{1,0:T(8,128)S(1)} copy-done((f32[16,128]{1,0:T(8,128)S(1)}, f32[16,128]{1,0:T(8,128)}, u32[]{:S(2)}) %copy-start.6) | copy-done | bytes 8216
  6.3 19.4 %shard_map.73 = f32[12,36,16,128]{3,2,1,0:T(8,128)S(1)} custom-call(f32[12,36,16,128]{3,2,1,0:T(8,128)S(1)} %copy-done, s32[64,128]{1,0:T(8,128)S(1)} %copy-done.1, s32[4,16,128]{2,1,0:T(8,128)S(1)} %copy-done.2, f32[16,128]{1,0:T(8,128)S(1)} %copy-done.3, f32[16,128]{1,0:T(8,128)S(1)} %copy-done.4, f32[16,128]{1,0:T(8,128)S(1)} %copy-done.5, ...), custom_call_target="tpu_custom_call" | custom-call | tf_op jit(solution)/shard_map/pallas_call | solution.py:319
  25.8 1.8 %copy.9 = f32[12,36,16,128]{3,2,1,0:T(8,128)} copy(f32[12,36,16,128]{3,2,1,0:T(8,128)S(1)} %shard_map.73) | data formatting | bytes 7077888
Async XLA Ops:
  0.0 2.0 %copy-start = (f32[12,36,16,128]{3,2,1,0:T(8,128)S(1)}, f32[12,36,16,128]{3,2,1,0:T(8,128)}, u32[]{:S(2)}) copy-start(f32[12,36,16,128]{3,2,1,0:T(8,128)} %spectra.1) | copy-start | bytes 10616836
  2.0 0.8 %copy-start.1 = (s32[64,128]{1,0:T(8,128)S(1)}, s32[64,128]{1,0:T(8,128)}, u32[]{:S(2)}) copy-start(s32[64,128]{1,0:T(8,128)} %mask_in.1) | copy-start | bytes 98308
  2.8 0.8 %copy-start.2 = (s32[4,16,128]{2,1,0:T(8,128)S(1)}, s32[4,16,128]{2,1,0:T(8,128)}, u32[]{:S(2)}) copy-start(s32[4,16,128]{2,1,0:T(8,128)} %nbr_in.1) | copy-start | bytes 98308
  3.5 0.7 %copy-start.3 = (f32[16,128]{1,0:T(8,128)S(1)}, f32[16,128]{1,0:T(8,128)}, u32[]{:S(2)}) copy-start(f32[16,128]{1,0:T(8,128)} %courant_in.1) | copy-start | bytes 24580
  4.2 0.7 %copy-start.4 = (f32[16,128]{1,0:T(8,128)S(1)}, f32[16,128]{1,0:T(8,128)}, u32[]{:S(2)}) copy-start(f32[16,128]{1,0:T(8,128)} %turning_in.1) | copy-start | bytes 24580
  4.9 0.7 %copy-start.5 = (f32[16,128]{1,0:T(8,128)S(1)}, f32[16,128]{1,0:T(8,128)}, u32[]{:S(2)}) copy-start(f32[16,128]{1,0:T(8,128)} %wspeed_in.1) | copy-start | bytes 24580
  5.6 0.7 %copy-start.6 = (f32[16,128]{1,0:T(8,128)S(1)}, f32[16,128]{1,0:T(8,128)}, u32[]{:S(2)}) copy-start(f32[16,128]{1,0:T(8,128)} %wdir_in.1) | copy-start | bytes 24580

commit v3 on v2

--- a/solution.py
+++ b/solution.py
@@ -345,7 +345,7 @@
                 dma((2, 2)), dma((2, 2)), dma((n_bands,)), dma((n_bands,)),
             ],
             compiler_params=pltpu.CompilerParams(
-                collective_id=0, has_side_effects=True, vmem_limit_bytes=40 * 1024 * 1024
+                collective_id=0, has_side_effects=True, vmem_limit_bytes=60 * 1024 * 1024
             ),
         )(spectra, sea_mask, neighbors, courant, turning, wind_speed, wind_dir)
 

time: 28 us -> 23.1 us (0.83); the launches traced: 27.6 us -> 23 us
  local copies, waits for them, and re-layouts: 8.1 us -> 4.02 us
  Pallas kernels: 19.4 us -> 19 us
    unnamed x15 -> x1, local copies, waits for them, and re-layouts: 8.1 us -> 4.02 us
    pallas_call x1, Pallas kernels: 19.4 us -> 19 us  [per_device(): pl.pallas_call(functools.partial(kernel, n_bands, n_tiles, bw, nd, tp, wi...]
where the time goes in v3:
time: 23.1 us; the launch traced here: 23 us
  Pallas kernels  19 us (82%)
  local copies, waits for them, and re-layouts  4.02 us (17%)
    pallas_call x1, Pallas kernels, per_device(): pl.pallas_call(functools.partial(kernel, n_bands, n_tiles, bw, nd, tp, wi...  19 us
    unnamed x1, local copies, waits for them, and re-layouts  4.02 us

profile of v3, /device:TPU:0, one launch (start us, length us, event | category | flops | bytes accessed | tf_op | source)
XLA Modules:
  0.0 23.0 jit_solution(1530883496878554361)
XLA Ops:
  0.0 19.0 %shard_map.73 = f32[12,36,16,128]{3,2,1,0:T(8,128)} custom-call(f32[12,36,16,128]{3,2,1,0:T(8,128)} %spectra.1, s32[64,128]{1,0:T(8,128)} %mask_in.1, s32[4,16,128]{2,1,0:T(8,128)} %nbr_in.1, f32[16,128]{1,0:T(8,128)} %courant_in.1, f32[16,128]{1,0:T(8,128)} %turning_in.1, f32[16,128]{1,0:T(8,128)} %wspeed_in.1, f32[16,128]{1,0:T(8,128)} %wdir_in.1), custom_call_target="tpu_custom_call" | custom-call | tf_op jit(solution)/shard_map/pallas_call | solution.py:319
  19.0 4.0 %copy.9 = f32[12,36,16,128]{3,2,1,0:T(8,128)} copy(f32[12,36,16,128]{3,2,1,0:T(8,128)} %shard_map.73) | data formatting | bytes 7077888

commit v4 on v3

--- a/solution.py
+++ b/solution.py
@@ -12,6 +12,9 @@
 F32 = jnp.float32
 LOG2E = 1.0 / math.log(2.0)
 GROUP = 2
+PIECES = 1
+STEP_VMEM = 56
+SOURCE_VMEM = 16
 
 
 def lane_gather(x, idx):
@@ -33,9 +36,10 @@
 
 def kernel(
     n_bands, n_tiles, bw, nd, tp, width,
-    spectra, mask_in, nbr_in, courant_in, turning_in, wspeed_in, wdir_in, out,
-    mask, nbr, courant, turning, wspeed, wdir, ext, e1, e2, obuf, ftab, mext, weights, lanes, hsend, hrecv, macc, mrecv,
-    small_sem, load_sem, out_sem, band_send, band_recv, tile_send, tile_recv,
+    spectra, mask_in, nbr_in, courant_in, turning_in, wspeed_in, wdir_in,
+    e2, ftab, gone,
+    mask, nbr, courant, turning, wspeed, wdir, ext, e1, mext, weights, lanes, hsend, hrecv, macc, mrecv,
+    small_sem, load_sem, band_send, band_recv, tile_send, tile_recv,
     diag_send, diag_recv, m_send, m_recv,
 ):
     band = lax.axis_index("bands")
@@ -71,23 +75,31 @@
         pl.semaphore_signal(
             barrier, inc=1, device_id={"bands": lax.rem(band + k, n_bands)}, device_id_type=MESH
         )
-    for dt in (1, n_tiles - 1):
-        for db in (0, 1, n_bands - 1):
-            pl.semaphore_signal(
-                barrier, inc=1,
-                device_id={
-                    "bands": lax.rem(band + db, n_bands), "tiles": lax.rem(tile + dt, n_tiles)
-                },
-                device_id_type=MESH,
-            )
-    pl.semaphore_wait(barrier, n_bands - 1 + 6)
-
-    def band_copy(side):
+    count = n_bands - 1
+    for side in (0, 1):
+        for dest, here in (
+            ({}, has_tile[side]),
+            ({"bands": band - 1}, has_tile[side] & has_band[0]),
+            ({"bands": band + 1}, has_tile[side] & has_band[1]),
+        ):
+            @pl.when(here)
+            def _(side=side, dest=dest):
+                pl.semaphore_signal(
+                    barrier, inc=1, device_id={"tiles": tile + step[side], **dest},
+                    device_id_type=MESH,
+                )
+            count = count + jnp.where(here, 1, 0)
+    pl.semaphore_wait(barrier, count)
+
+    piece = nd // PIECES
+
+    def band_copy(side, n):
         first, place = (bw - 2, 0) if side == 0 else (0, bw + 2)
+        u, d = n // PIECES, n % PIECES * piece
         return pltpu.make_async_remote_copy(
-            src_ref=spectra.at[first : first + 2],
-            dst_ref=ext.at[place : place + 2, :, 8 : 8 + tp, :],
-            send_sem=band_send.at[side], recv_sem=band_recv.at[side],
+            src_ref=spectra.at[first + u, d : d + piece],
+            dst_ref=ext.at[place + u, d : d + piece, 8 : 8 + tp, :],
+            send_sem=band_send.at[side, n], recv_sem=band_recv.at[side, n],
             device_id={"bands": band - step[side]}, device_id_type=MESH,
         )
 
@@ -120,7 +132,8 @@
     for side in (0, 1):
         @pl.when(has_band[1 - side])
         def _(side=side):
-            band_copy(side).start()
+            for n in range(2 * PIECES):
+                band_copy(side, n).start()
 
     for g in range(groups):
         for i in range(g * GROUP, (g + 1) * GROUP):
@@ -243,7 +256,8 @@
     for bside, place in ((0, 0), (1, bw + 2)):
         @pl.when(has_band[bside])
         def _(bside=bside, place=place):
-            band_copy(bside).wait_recv()
+            for n in range(2 * PIECES):
+                band_copy(bside, n).wait_recv()
             for side in (0, 1):
                 @pl.when(has_tile[side])
                 def _(side=side):
@@ -265,7 +279,28 @@
         m_copy(k).wait()
         m_sum = m_sum + mrecv[k]
     m_sum = m_sum * (1.0 / (nf * nd))
-    mrecv[0] = LOG2E * (m_sum / (m_sum + 1.0))
+    gone[...] = LOG2E * (m_sum / (m_sum + 1.0))
+
+    for side in (0, 1):
+        @pl.when(has_band[1 - side])
+        def _(side=side):
+            for n in range(2 * PIECES):
+                band_copy(side, n).wait_send()
+
+        @pl.when(has_tile[1 - side])
+        def _(side=side):
+            for g in range(groups):
+                tile_copy(side, g).wait_send()
+
+        for bside in (0, 1):
+            @pl.when(has_tile[1 - side] & has_band[1 - bside])
+            def _(side=side, bside=bside):
+                diag_copy(bside, side).wait_send()
+
+
+def source_kernel(n_bands, bw, nd, tp, e2, ftab, gone, out, obuf, out_sem):
+    band = lax.axis_index("bands")
+    nf = n_bands * bw
 
     def store(i):
         return pltpu.make_async_copy(obuf.at[i], out.at[i], out_sem.at[i])
@@ -276,7 +311,7 @@
         k = 0.05 * (1.0 + fraction)
         for h in range(0, tp, 8):
             here = pl.ds(h, 8)
-            damping = (0.2 + fraction) * mrecv[0, here, :]
+            damping = (0.2 + fraction) * gone[here, :]
             for j in range(nd):
                 up, down = (j + 3) % nd, (j - 3) % nd
                 a1, a2 = e2[i + 4, up, here, :], e2[i + 4, down, here, :]
@@ -292,20 +327,6 @@
 
     for i in range(bw):
         store(i).wait()
-    for side in (0, 1):
-        @pl.when(has_band[1 - side])
-        def _(side=side):
-            band_copy(side).wait_send()
-
-        @pl.when(has_tile[1 - side])
-        def _(side=side):
-            for g in range(groups):
-                tile_copy(side, g).wait_send()
-
-        for bside in (0, 1):
-            @pl.when(has_tile[1 - side] & has_band[1 - bside])
-            def _(side=side, bside=bside):
-                diag_copy(bside, side).wait_send()
 
 
 def solution(mesh):
@@ -316,11 +337,16 @@
         hbm = pl.BlockSpec(memory_space=pltpu.HBM)
         groups = bw // GROUP
         dma = pltpu.SemaphoreType.DMA
-        return pl.pallas_call(
+        vmem = pl.BlockSpec(memory_space=pltpu.VMEM)
+        stepped = pl.pallas_call(
             functools.partial(kernel, n_bands, n_tiles, bw, nd, tp, width),
-            out_shape=jax.ShapeDtypeStruct(spectra.shape, F32),
+            out_shape=[
+                pltpu.VMEM((bw + 4, nd, tp, width), F32),
+                pltpu.VMEM((nd, tp, width), F32),
+                pltpu.VMEM((tp, width), F32),
+            ],
             in_specs=[hbm] * 7,
-            out_specs=hbm,
+            out_specs=[vmem] * 3,
             scratch_shapes=[
                 pltpu.VMEM(sea_mask.shape, jnp.int32),
                 pltpu.VMEM(neighbors.shape, jnp.int32),
@@ -329,9 +355,6 @@
                 pltpu.VMEM((tp, width), F32),
                 pltpu.VMEM((tp, width), F32),
                 pltpu.VMEM((bw + 4, nd, tp + 16, width), F32),
-                pltpu.VMEM((nd, tp, width), F32),
-                pltpu.VMEM((bw + 4, nd, tp, width), F32),
-                pltpu.VMEM((bw, nd, tp, width), F32),
                 pltpu.VMEM((nd, tp, width), F32),
                 pltpu.VMEM((tp + 16, width), F32),
                 pltpu.VMEM((5, tp, width), F32),
@@ -340,14 +363,22 @@
                 pltpu.VMEM((2, (bw + 4) * nd, width), F32),
                 pltpu.VMEM((tp, width), F32),
                 pltpu.VMEM((n_bands, tp, width), F32),
-                dma((6,)), dma((bw,)), dma((bw,)), dma((2,)), dma((2,)),
+                dma((6,)), dma((bw,)), dma((2, 2 * PIECES)), dma((2, 2 * PIECES)),
                 dma((2, groups)), dma((2, groups)),
                 dma((2, 2)), dma((2, 2)), dma((n_bands,)), dma((n_bands,)),
             ],
             compiler_params=pltpu.CompilerParams(
-                collective_id=0, has_side_effects=True, vmem_limit_bytes=60 * 1024 * 1024
+                collective_id=0, has_side_effects=True, vmem_limit_bytes=STEP_VMEM * 1024 * 1024
             ),
         )(spectra, sea_mask, neighbors, courant, turning, wind_speed, wind_dir)
+        return pl.pallas_call(
+            functools.partial(source_kernel, n_bands, bw, nd, tp),
+            out_shape=jax.ShapeDtypeStruct(spectra.shape, F32),
+            in_specs=[vmem] * 3,
+            out_specs=pl.BlockSpec(memory_space=pl.ANY),
+            scratch_shapes=[pltpu.VMEM((bw, nd, tp, width), F32), dma((bw,))],
+            compiler_params=pltpu.CompilerParams(vmem_limit_bytes=SOURCE_VMEM * 1024 * 1024),
+        )(*stepped)
 
     placed = (
         P("bands", None, ("runs", "tiles"), None),

time: 23.1 us -> 19.1 us (0.83)
  local copies, waits for them, and re-layouts: 4.02 us -> 0 us
    unnamed x1 -> x0, local copies, waits for them, and re-layouts: 4.02 us -> none
    pallas_call x0 -> x1, Pallas kernels: none -> 2.66 us  [per_device(): pl.pallas_call(functools.partial(source_kernel, n_bands, bw, nd, tp), out...]
    pallas_call x1, Pallas kernels: 19 us -> 16.3 us  [per_device(): pl.pallas_call(functools.partial(kernel, n_bands, n_tiles, bw, nd, tp, wi...]
where the time goes in v4:
time: 19.1 us; the launch traced here: 19 us
  Pallas kernels  19 us (99%)
    pallas_call x1, Pallas kernels, per_device(): pl.pallas_call(functools.partial(kernel, n_bands, n_tiles, bw, nd, tp, wi...  16.3 us
    pallas_call x1, Pallas kernels, per_device(): pl.pallas_call(functools.partial(source_kernel, n_bands, bw, nd, tp), out...  2.66 us

profile of v4, /device:TPU:0, one launch (start us, length us, event | category | flops | bytes accessed | tf_op | source)
XLA Modules:
  0.0 19.0 jit_solution(5933531289846393876)
XLA Ops:
  0.0 16.3 %shard_map.73 = (f32[16,36,16,128]{3,2,1,0:T(8,128)S(1)}, f32[36,16,128]{2,1,0:T(8,128)S(1)}, f32[16,128]{1,0:T(8,128)S(1)}) custom-call(f32[12,36,16,128]{3,2,1,0:T(8,128)} %spectra.1, s32[64,128]{1,0:T(8,128)} %mask_in.1, s32[4,16,128]{2,1,0:T(8,128)} %nbr_in.1, f32[16,128]{1,0:T(8,128)} %courant_in.1, f32[16,128]{1,0:T(8,128)} %turning_in.1, ...), custom_call_target="tpu_custom_call" | custom-call | tf_op jit(solution)/shard_map/pallas_call | solution.py:341
  16.3 2.7 %shard_map.74 = f32[12,36,16,128]{3,2,1,0:T(8,128)} custom-call(f32[16,36,16,128]{3,2,1,0:T(8,128)S(1)} %get-tuple-element.8.e2, f32[36,16,128]{2,1,0:T(8,128)S(1)} %get-tuple-element.9.ftab, f32[16,128]{1,0:T(8,128)S(1)} %get-tuple-element.10.gone), custom_call_target="tpu_custom_call" | custom-call | tf_op jit(solution)/shard_map/pallas_call | solution.py:374

commit v5 on v4

--- a/solution.py
+++ b/solution.py
@@ -13,7 +13,7 @@
 LOG2E = 1.0 / math.log(2.0)
 GROUP = 2
 PIECES = 1
-STEP_VMEM = 56
+STEP_VMEM = 52
 SOURCE_VMEM = 16
 
 
@@ -37,7 +37,7 @@
 def kernel(
     n_bands, n_tiles, bw, nd, tp, width,
     spectra, mask_in, nbr_in, courant_in, turning_in, wspeed_in, wdir_in,
-    e2, ftab, gone,
+    e2, ftab, gone, inner,
     mask, nbr, courant, turning, wspeed, wdir, ext, e1, mext, weights, lanes, hsend, hrecv, macc, mrecv,
     small_sem, load_sem, band_send, band_recv, tile_send, tile_recv,
     diag_send, diag_recv, m_send, m_recv,
@@ -253,6 +253,18 @@
     for k in range(1, n_bands):
         m_copy(k).start()
 
+    def interior(i, carry):
+        fraction = (band * bw + i).astype(F32) * (1.0 / (nf - 1))
+        for h in range(0, tp, 8):
+            here = pl.ds(h, 8)
+            for j in range(nd):
+                inner[i - 2, j, here, :] = transfer(
+                    e2, i, j, nd, here, 0.05 * (1.0 + fraction)
+                )
+        return carry
+
+    lax.fori_loop(2, bw - 2, interior, 0)
+
     for bside, place in ((0, 0), (1, bw + 2)):
         @pl.when(has_band[bside])
         def _(bside=bside, place=place):
@@ -298,32 +310,42 @@
                 diag_copy(bside, side).wait_send()
 
 
-def source_kernel(n_bands, bw, nd, tp, e2, ftab, gone, out, obuf, out_sem):
+def transfer(e2, i, j, nd, here, k):
+    up, down = (j + 3) % nd, (j - 3) % nd
+    a1, a2 = e2[i + 4, up, here, :], e2[i + 4, down, here, :]
+    b1, b2 = e2[i, down, here, :], e2[i, up, here, :]
+    mid = e2[i + 2, j, here, :]
+    return (k * mid) * (mid * ((a1 + b1) + (a2 + b2)) - 2.0 * (a1 * b1 + a2 * b2))
+
+
+def source_kernel(n_bands, bw, nd, tp, e2, ftab, gone, inner, out, obuf, out_sem):
     band = lax.axis_index("bands")
     nf = n_bands * bw
 
     def store(i):
         return pltpu.make_async_copy(obuf.at[i], out.at[i], out_sem.at[i])
 
-    def finish(i, carry):
-        index = (band * bw + i).astype(F32)
-        fraction = index * (1.0 / (nf - 1))
+    def finish(i, ready):
+        fraction = (band * bw + i).astype(F32) * (1.0 / (nf - 1))
         k = 0.05 * (1.0 + fraction)
         for h in range(0, tp, 8):
             here = pl.ds(h, 8)
             damping = (0.2 + fraction) * gone[here, :]
             for j in range(nd):
-                up, down = (j + 3) % nd, (j - 3) % nd
-                a1, a2 = e2[i + 4, up, here, :], e2[i + 4, down, here, :]
-                b1, b2 = e2[i, down, here, :], e2[i, up, here, :]
-                mid = e2[i + 2, j, here, :]
                 gain = jnp.exp2(fraction * ftab[j, here, :] - damping)
-                inner = mid * ((a1 + b1) + (a2 + b2)) - 2.0 * (a1 * b1 + a2 * b2)
-                obuf[i, j, here, :] = mid * (gain + k * inner)
+                if ready:
+                    extra = inner[i - 2, j, here, :]
+                else:
+                    extra = transfer(e2, i, j, nd, here, k)
+                obuf[i, j, here, :] = e2[i + 2, j, here, :] * gain + extra
         store(i).start()
-        return carry
-
-    lax.fori_loop(0, bw, finish, 0)
+
+    for low, high, ready in ((0, 2, False), (bw - 2, bw, False), (2, bw - 2, True)):
+        def one(i, carry, ready=ready):
+            finish(i, ready)
+            return carry
+
+        lax.fori_loop(low, high, one, 0)
 
     for i in range(bw):
         store(i).wait()
@@ -344,9 +366,10 @@
                 pltpu.VMEM((bw + 4, nd, tp, width), F32),
                 pltpu.VMEM((nd, tp, width), F32),
                 pltpu.VMEM((tp, width), F32),
+                pltpu.VMEM((bw - 4, nd, tp, width), F32),
             ],
             in_specs=[hbm] * 7,
-            out_specs=[vmem] * 3,
+            out_specs=[vmem] * 4,
             scratch_shapes=[
                 pltpu.VMEM(sea_mask.shape, jnp.int32),
                 pltpu.VMEM(neighbors.shape, jnp.int32),
@@ -374,7 +397,7 @@
         return pl.pallas_call(
             functools.partial(source_kernel, n_bands, bw, nd, tp),
             out_shape=jax.ShapeDtypeStruct(spectra.shape, F32),
-            in_specs=[vmem] * 3,
+            in_specs=[vmem] * 4,
             out_specs=pl.BlockSpec(memory_space=pl.ANY),
             scratch_shapes=[pltpu.VMEM((bw, nd, tp, width), F32), dma((bw,))],
             compiler_params=pltpu.CompilerParams(vmem_limit_bytes=SOURCE_VMEM * 1024 * 1024),

time: 19.1 us -> 18.7 us (0.979)
  Pallas kernels: 19 us -> 18.6 us
    pallas_call x1, Pallas kernels: 2.66 us -> 2.26 us  [per_device(): pl.pallas_call(functools.partial(source_kernel, n_bands, bw, nd, tp), out...]
where the time goes in v5:
time: 18.7 us; the launch traced here: 18.6 us
  Pallas kernels  18.6 us (99%)
    pallas_call x1, Pallas kernels, per_device(): pl.pallas_call(functools.partial(kernel, n_bands, n_tiles, bw, nd, tp, wi...  16.3 us
    pallas_call x1, Pallas kernels, per_device(): pl.pallas_call(functools.partial(source_kernel, n_bands, bw, nd, tp), out...  2.26 us

profile of v5, /device:TPU:0, one launch (start us, length us, event | category | flops | bytes accessed | tf_op | source)
XLA Modules:
  0.0 18.6 jit_solution(13559584884314031104)
XLA Ops:
  0.0 16.3 %shard_map.73 = (f32[16,36,16,128]{3,2,1,0:T(8,128)S(1)}, f32[36,16,128]{2,1,0:T(8,128)S(1)}, f32[16,128]{1,0:T(8,128)S(1)}, f32[8,36,16,128]{3,2,1,0:T(8,128)S(1)}) custom-call(f32[12,36,16,128]{3,2,1,0:T(8,128)} %spectra.1, s32[64,128]{1,0:T(8,128)} %mask_in.1, s32[4,16,128]{2,1,0:T(8,128)} %nbr_in.1, f32[16,128]{1,0:T(8,128)} %courant_in.1, ...), custom_call_target="tpu_custom_call" | custom-call | tf_op jit(solution)/shard_map/pallas_call | solution.py:363
  16.3 2.3 %shard_map.74 = f32[12,36,16,128]{3,2,1,0:T(8,128)} custom-call(f32[16,36,16,128]{3,2,1,0:T(8,128)S(1)} %get-tuple-element.9.e2, f32[36,16,128]{2,1,0:T(8,128)S(1)} %get-tuple-element.10.ftab, f32[16,128]{1,0:T(8,128)S(1)} %get-tuple-element.11.gone, f32[8,36,16,128]{3,2,1,0:T(8,128)S(1)} %get-tuple-element.12.inner), custom_call_target="tpu_custom_call" | custom-call | tf_op jit(solution)/shard_map/pallas_call | solution.py:397
